TPU v7x, 32 devices: a whole 2x2x4 slice. The times are simulated.
32 devices in a mesh: grp: 2 (over x), query: 16 (over z, y, core).
Axes of the slice: x: 2, y: 2, z: 4, core: 2. Of those that a mesh axis runs over, the one named last changes fastest.
Arguments:
- acts: bfloat16 [8192, 8192], P(('grp', 'query')), parts along dimension 0, may hold values from -6 to 6
- grads: bfloat16 [8192, 14336], P(('grp', 'query')), parts along dimension 0, may hold values from -6 to 6
- u_factor: bfloat16 [28672, 512], P(('grp', 'query')), parts along dimension 0, may hold values from -0.00018310547 to 0.00018310547
- v_factor: bfloat16 [16384, 512], P(('grp', 'query')), parts along dimension 0, may hold values from -0.0625 to 0.0625
- lengths: int32 [4], P('grp'), parts along dimension 0, may hold values from 1 to 2048, 3072 in all
Outputs:
- scores: float32 [32, 2], P('grp'), parts along dimension 0
There are 2 independent parts, one for each index of `grp`. A program takes and returns all parts, laid end to end along the dimension named above; each array names one. Nothing has to cross between parts.
Inputs may be any that keep to these rules, and one draw needn't show every extreme that they name: Sequence s owns token slots s * 2048 to (s + 1) * 2048 - 1, of which the first lengths[s] are live; the counts sum to three quarters of 4096.
All inputs are finite; a program needn't handle non-finite values.
Results may differ from a plain program's by a relative error of at most 0.0003.
Values may be sent and summed in bfloat16 or wider, within the bound.
A program may use at most 128 MiB of HBM per device.

v0:
```python
import jax
import jax.numpy as jnp
from jax import lax
from jax.sharding import PartitionSpec as P

RANK = 32
LENGTH = 2048


def shards(acts, grads, u_factor, v_factor, lengths):
    rows_here = acts.shape[0]
    members = lax.axis_size("query")
    factor_cols = u_factor.shape[1]
    grads_blocks = grads.reshape(rows_here, members, u_factor.shape[0])
    acts_blocks = acts.reshape(rows_here, members, v_factor.shape[0])
    u_stack = u_factor[None]
    v_stack = v_factor[None]
    u_whole, v_whole = (
        lax.all_gather(u_stack, "query", axis=0, tiled=True),
        lax.all_gather(v_stack, "query", axis=0, tiled=True),
    )
    out_proj = jnp.einsum("tkf,kfc->tc", grads_blocks, u_whole, preferred_element_type=jnp.float32)
    in_proj = jnp.einsum("tkf,kfc->tc", acts_blocks, v_whole, preferred_element_type=jnp.float32)
    token_score = (out_proj * in_proj).reshape(rows_here, factor_cols // RANK, RANK).sum(axis=2)
    first_slot = lax.axis_index("query") * rows_here
    seq_here = first_slot // LENGTH
    offsets = first_slot % LENGTH + jnp.arange(rows_here, dtype=jnp.int32)
    seq_count = lengths.shape[0]
    seq_ids = jnp.arange(seq_count, dtype=jnp.int32)
    selector = seq_ids == seq_here
    live_count = jnp.sum(jnp.where(selector, lengths, jnp.zeros_like(lengths)))
    live = (offsets < live_count).astype(jnp.float32)
    query_sums = jnp.sum(token_score * live[:, None], axis=0)
    partial_value = query_sums[:, None] * selector.astype(jnp.float32)[None, :]
    return lax.psum(partial_value, "query")


def solution(mesh):
    return jax.shard_map(
        shards,
        mesh=mesh,
        in_specs=(
            P(("grp", "query"), None),
            P(("grp", "query"), None),
            P(("grp", "query"), None),
            P(("grp", "query"), None),
            P("grp"),
        ),
        out_specs=P("grp", None),
        check_vma=False,
    )
```

profile of v0, /device:TPU:0, one launch (start us, length us, event | category | flops | bytes accessed | tf_op | source)
XLA Modules:
  0.0 247.3 jit_solution(5894753123292556120)
XLA Ops:
  6.5 0.0 all-gather.5.cloned.1.call-start
  6.5 0.7 all-gather.5.cloned.1.call-update
  7.3 0.0 all-gather.7.cloned.1.call-start
  7.3 0.7 all-gather.7.cloned.1.call-update
  8.0 1.3 fusion.15
  9.3 0.6 compare_convert_fusion
  10.0 116.2 %all-gather.5.cloned.1.call-done = bf16[14336,512]{1,0:T(8,128)(2,1)} async-done(((bf16[896,512]{1,0:T(8,128)(2,1)}), bf16[14336,512]{1,0:T(8,128)(2,1)}) %all-gather.5.cloned.1.call-update) | async-done | bytes 14680080 | tf_op jit(solution)/shard_map/all_gather | solution.py:19
  126.2 9.3 %fusion.12 = f32[256,512]{1,0:T(8,128)S(1)} fusion(bf16[16,896,512]{2,1,0:T(8,128)(2,1)} %bitcast.26, bf16[32,16,8,896]{3,2,1,0:T(8,128)(2,1)} %bitcast.28), kind=kOutput, calls=%fused_computation.8 | convolution fusion | flops 3758096384 | bytes 22544384 | tf_op jit(solution)/shard_map/tkf,kfc->tc/dot_general | solution.py:22
  135.6 65.9 %all-gather.7.cloned.1.call-done = bf16[8192,512]{1,0:T(8,128)(2,1)} async-done(((bf16[512,512]{1,0:T(8,128)(2,1)}), bf16[8192,512]{1,0:T(8,128)(2,1)}) %all-gather.7.cloned.1.call-update) | async-done | bytes 8388624 | tf_op jit(solution)/shard_map/all_gather | solution.py:20
  201.5 7.0 %fusion.9 = f32[256,512]{1,0:T(8,128)S(1)} fusion(f32[256,512]{1,0:T(8,128)S(1)} %fusion.12, bf16[16,512,512]{2,1,0:T(8,128)(2,1)} %bitcast.27, bf16[32,16,8,512]{3,2,1,0:T(8,128)(2,1)} %bitcast.29), kind=kOutput, calls=%fused_computation.7 | convolution fusion | flops 2147614720 | bytes 13631488 | tf_op jit(solution)/shard_map/tkf,kfc->tc/dot_general | solution.py:23
  208.5 0.2 copy.13
  208.7 0.1 bitcast_reduce_fusion
  208.8 0.1 multiply_reduce_fusion
  208.9 0.1 broadcast_multiply_fusion
  208.9 31.5 %psum.7 = f32[16,2]{0,1:T(2,128)} all-reduce(f32[16,2]{0,1:T(2,128)S(1)} %broadcast_multiply_fusion), channel_id=1, replica_groups=mesh['grp'=2,'query'=16] {'query'}, use_global_device_ids=true, to_apply=%region_3.4 | all-reduce | flops 32 | bytes 256 | tf_op jit(solution)/shard_map/psum | solution.py:35
  (1 shorter events, 0.0 us)
Async XLA Ops:
  6.5 119.7 %all-gather.5.cloned.1.call-start = ((), (), s32[]{:S(2)}) async-start(), calls=%async_computation | async-start | bytes 15597568 | tf_op jit(solution)/shard_map/all_gather | solution.py:19
  7.3 194.2 %all-gather.7.cloned.1.call-start = ((), (), s32[]{:S(2)}) async-start(), calls=%async_computation.1 | async-start | bytes 8912896 | tf_op jit(solution)/shard_map/all_gather | solution.py:20
Sparse Core Ops, SparseCore 0:
  9.7 116.5 all-gather.4
  128.4 73.0 all-gather.6
where the time goes:
time: 247 us
  waiting for transfers between devices  184 us (74%)
  blocking collectives  31.5 us (13%)
  matrix products  16.3 us (7%)
  between operations  13.5 us (5%)
    all_gather x1, waiting for transfers between devices, shards(): lax.all_gather(u_stack, 'query', axis=0, tiled=True)  116 us
    all_gather x1, waiting for transfers between devices, shards(): lax.all_gather(v_stack, 'query', axis=0, tiled=True)  65.9 us
    psum x1, blocking collectives, shards(): return lax.psum(partial_value, 'query')  31.5 us
    dot_general x1, matrix products, shards(): jnp.einsum('tkf,kfc->tc', grads_blocks, u_whole, preferred_element_type=j...  9.35 us
    dot_general x1, matrix products, shards(): jnp.einsum('tkf,kfc->tc', acts_blocks, v_whole, preferred_element_type=jn...  6.98 us
  transfers between devices with their start and end apart: 2, of which 2 were waited for; matrix products, arithmetic and copies ran while one was open for 5% of the time, Pallas kernels for 0%

commit v1 on v0

v1 whole, which is shorter than its diff:
```python
import functools

import jax
import jax.numpy as jnp
from jax import lax
from jax.experimental import pallas as pl
from jax.experimental.pallas import tpu as pltpu
from jax.sharding import PartitionSpec as P

RANK = 32
LENGTH = 2048
MESH = pl.DeviceIdType.MESH
DEPTH, WIDTH, CORES = 4, 2, 2
UP, DOWN, ACROSS, SIBLING = range(4)


def device(z, y, core):
    return (z * WIDTH + y) * CORES + core


def nearest(z, rank):
    near = jnp.where(z < 2, z, 3 - z)
    swapped = jnp.where(rank == 0, 1, jnp.where(rank == 1, 0, rank))
    found = jnp.where(near == 0, rank, swapped)
    return jnp.where(z < 2, found, 3 - found)


def kernel(pieces, lengths, grads, acts, u_own, v_own, out, u_all, v_all, grads_here, acts_here, out_proj, in_proj,
           parts, load_sem, send_sem, recv_sem, part_send_sem, part_recv_sem):
    me = lax.axis_index("query")
    members = u_all.shape[0]
    core = lax.rem(me, CORES)
    y = lax.rem(me // CORES, WIDTH)
    z = me // (CORES * WIDTH)
    sibling = device(z, y, 1 - core)
    across = device(z, 1 - y, core)
    u_rows, v_rows = u_own.shape[0], v_own.shape[0]
    rows = grads.shape[0]

    loads = [
        pltpu.make_async_copy(u_own, u_all.at[me], load_sem.at[0]),
        pltpu.make_async_copy(v_own, v_all.at[me], load_sem.at[1]),
        pltpu.make_async_copy(grads, grads_here, load_sem.at[2]),
        pltpu.make_async_copy(acts, acts_here, load_sem.at[3]),
    ]
    for load in loads:
        load.start()

    barrier = pltpu.get_barrier_semaphore()

    @pl.loop(1, members)
    def _(step):
        pl.semaphore_signal(barrier, inc=1, device_id={"query": lax.rem(me + step, members)}, device_id_type=MESH)

    pl.semaphore_wait(barrier, members - 1)

    def piece(owner, kind):
        side, start, size = pieces[kind]
        return (u_all if side == 0 else v_all).at[owner, pl.ds(start, size)]

    def copy(owner, kind, way, target):
        return pltpu.make_async_remote_copy(
            src_ref=piece(owner, kind),
            dst_ref=piece(owner, kind),
            send_sem=send_sem.at[way, owner, kind],
            recv_sem=recv_sem.at[owner, kind],
            device_id={"query": target},
            device_id_type=MESH,
        )

    def start(one):
        one.start()

    def drain(one):
        one.wait_send()

    def arrived(owner, kind):
        copy(owner, kind, SIBLING, sibling).wait_recv()

    last = len(pieces) - 1
    direct = tuple(range(last))

    def along(act, owner, kind, up, down):
        @pl.when(up)
        def _():
            act(copy(owner, kind, UP, device(z + 1, y, core)))

        @pl.when(down)
        def _():
            act(copy(owner, kind, DOWN, device(z - 1, y, core)))

    def over(act, owner, kind):
        act(copy(owner, kind, ACROSS, across))

    def beside(act, owner, kind):
        act(copy(owner, kind, SIBLING, sibling))

    def send_own(act):
        up, down = z < DEPTH - 1, z > 0
        over(act, me, last)
        along(act, me, last, up, down)
        for kind in direct:
            along(act, me, kind, up, down)
            over(act, me, kind)
        for kind in range(last + 1):
            beside(act, me, kind)

    def send_neighbours(act, wait):
        wait(across, last)
        along(act, across, last, z < DEPTH - 1, z > 0)
        beside(act, across, last)

    def send_line(act, wait, rank):
        other = nearest(z, rank)
        up = jnp.logical_and(other < z, z < DEPTH - 1)
        down = jnp.logical_and(other > z, z > 0)
        same, opposite = device(other, y, core), device(other, 1 - y, core)
        wait(same, last)
        along(act, same, last, up, down)
        beside(act, same, last)
        for kind in direct:
            wait(same, kind)
            along(act, same, kind, up, down)
            over(act, same, kind)
            beside(act, same, kind)
        wait(opposite, last)
        along(act, opposite, last, up, down)
        beside(act, opposite, last)

    def send_crossed(act, wait, rank):
        opposite = device(nearest(z, rank), 1 - y, core)
        for kind in direct:
            wait(opposite, kind)
            beside(act, opposite, kind)

    def multiply(owner):
        u_columns = pl.ds(pl.multiple_of(owner * u_rows, 128), u_rows)
        v_columns = pl.ds(pl.multiple_of(owner * v_rows, 128), v_rows)
        out_proj[...] += jnp.dot(grads_here[:, u_columns], u_all[owner], preferred_element_type=jnp.float32)
        in_proj[...] += jnp.dot(acts_here[:, v_columns], v_all[owner], preferred_element_type=jnp.float32)

    def multiply_chip(other_z, other_y):
        @pl.loop(0, CORES)
        def _(turn):
            owner = device(other_z, other_y, jnp.where(turn == 0, core, 1 - core))

            @pl.when(turn == 1)
            def _():
                for kind in range(last + 1):
                    arrived(owner, kind)

            multiply(owner)

    loads[0].wait()
    loads[1].wait()
    send_own(start)
    out_proj[...] = jnp.zeros_like(out_proj)
    in_proj[...] = jnp.zeros_like(in_proj)
    send_neighbours(start, arrived)
    loads[2].wait()
    loads[3].wait()
    multiply_chip(z, y)

    @pl.loop(1, DEPTH)
    def _(rank):
        send_line(start, arrived, rank)
        send_crossed(start, arrived, rank - 1)
        multiply_chip(nearest(z, rank - 1), 1 - y)
        multiply_chip(nearest(z, rank), y)

    send_crossed(start, arrived, DEPTH - 1)
    multiply_chip(nearest(z, DEPTH - 1), 1 - y)

    first_slot = me * rows
    live_count = lengths[first_slot // LENGTH]
    offsets = lax.rem(first_slot, LENGTH) + lax.broadcasted_iota(jnp.int32, out_proj.shape, 0)
    product = out_proj[...] * in_proj[...]
    parts[me] = jnp.sum(jnp.where(offsets < live_count, product, 0.0), axis=0, keepdims=True)

    def part_copy(step):
        target = lax.rem(me + step, members)
        return pltpu.make_async_remote_copy(
            src_ref=parts.at[me],
            dst_ref=parts.at[me],
            send_sem=part_send_sem.at[step],
            recv_sem=part_recv_sem.at[step],
            device_id={"query": target},
            device_id_type=MESH,
        )

    @pl.loop(1, members)
    def _(step):
        part_copy(step).start()

    def no_wait(owner, kind):
        pass

    send_own(drain)
    send_neighbours(drain, no_wait)

    @pl.loop(1, DEPTH)
    def _(rank):
        send_line(drain, no_wait, rank)

    @pl.loop(0, DEPTH)
    def _(rank):
        send_crossed(drain, no_wait, rank)

    @pl.loop(1, members)
    def _(step):
        part_copy(step).wait()

    query_count, seq_count = out.shape
    shape = (query_count, parts.shape[2])
    mine = lax.broadcasted_iota(jnp.int32, shape, 1) // RANK == lax.broadcasted_iota(jnp.int32, shape, 0)
    columns = []
    for seq in range(seq_count):
        total = sum(parts[owner] for owner in range(members) if owner * rows // LENGTH == seq)
        columns.append(jnp.sum(jnp.where(mine, total, 0.0), axis=1, keepdims=True))
    out[...] = jnp.concatenate(columns, axis=1)


def fused(acts, grads, u_factor, v_factor, lengths):
    members = lax.axis_size("query")
    rows, factor_cols = acts.shape[0], u_factor.shape[1]
    u_rows, v_rows = u_factor.shape[0], v_factor.shape[0]
    u_cut = -(-u_rows // 256) * 128
    v_cut = v_rows // 256 * 128
    pieces = ((0, 0, u_cut), (0, u_cut, u_rows - u_cut), (1, 0, v_cut), (1, v_cut, v_rows - v_cut))
    hbm = pl.BlockSpec(memory_space=pl.ANY)
    return pl.pallas_call(
        functools.partial(kernel, pieces),
        out_shape=jax.ShapeDtypeStruct((factor_cols // RANK, lengths.shape[0]), jnp.float32),
        in_specs=[pl.BlockSpec(memory_space=pltpu.SMEM), hbm, hbm, hbm, hbm],
        out_specs=pl.BlockSpec(memory_space=pltpu.VMEM),
        scratch_shapes=[
            pltpu.VMEM((members, u_rows, factor_cols), u_factor.dtype),
            pltpu.VMEM((members, v_rows, factor_cols), v_factor.dtype),
            pltpu.VMEM(grads.shape, grads.dtype),
            pltpu.VMEM(acts.shape, acts.dtype),
            pltpu.VMEM((rows, factor_cols), jnp.float32),
            pltpu.VMEM((rows, factor_cols), jnp.float32),
            pltpu.VMEM((members, 1, factor_cols), jnp.float32),
            pltpu.SemaphoreType.DMA((4,)),
            pltpu.SemaphoreType.DMA((4, members, len(pieces))),
            pltpu.SemaphoreType.DMA((members, len(pieces))),
            pltpu.SemaphoreType.DMA((members,)),
            pltpu.SemaphoreType.DMA((members,)),
        ],
        compiler_params=pltpu.CompilerParams(
            collective_id=0, has_side_effects=True, vmem_limit_bytes=56 * 1024 * 1024
        ),
        cost_estimate=pl.CostEstimate(
            flops=2 * rows * factor_cols * members * (u_rows + v_rows),
            bytes_accessed=2 * (acts.size + grads.size + u_factor.size + v_factor.size),
            transcendentals=0,
        ),
    )(lengths, grads, acts, u_factor, v_factor)


def gathered(acts, grads, u_factor, v_factor, lengths):
    rows_here = acts.shape[0]
    members = lax.axis_size("query")
    factor_cols = u_factor.shape[1]
    grads_blocks = grads.reshape(rows_here, members, u_factor.shape[0])
    acts_blocks = acts.reshape(rows_here, members, v_factor.shape[0])
    u_whole = lax.all_gather(u_factor[None], "query", axis=0, tiled=True)
    v_whole = lax.all_gather(v_factor[None], "query", axis=0, tiled=True)
    out_proj = jnp.einsum("tkf,kfc->tc", grads_blocks, u_whole, preferred_element_type=jnp.float32)
    in_proj = jnp.einsum("tkf,kfc->tc", acts_blocks, v_whole, preferred_element_type=jnp.float32)
    token_score = (out_proj * in_proj).reshape(rows_here, factor_cols // RANK, RANK).sum(axis=2)
    first_slot = lax.axis_index("query") * rows_here
    offsets = first_slot % LENGTH + jnp.arange(rows_here, dtype=jnp.int32)
    selector = jnp.arange(lengths.shape[0], dtype=jnp.int32) == first_slot // LENGTH
    live_count = jnp.sum(jnp.where(selector, lengths, jnp.zeros_like(lengths)))
    live = (offsets < live_count).astype(jnp.float32)
    query_sums = jnp.sum(token_score * live[:, None], axis=0)
    return lax.psum(query_sums[:, None] * selector.astype(jnp.float32)[None, :], "query")


def solution(mesh):
    whole_grid = mesh.shape["query"] == DEPTH * WIDTH * CORES
    return jax.shard_map(
        fused if whole_grid else gathered,
        mesh=mesh,
        in_specs=(
            P(("grp", "query"), None),
            P(("grp", "query"), None),
            P(("grp", "query"), None),
            P(("grp", "query"), None),
            P("grp"),
        ),
        out_specs=P("grp", None),
        check_vma=False,
    )
```

time: 247 us -> 143 us (0.58)
  waiting for transfers between devices: 184 us -> 0 us
  Pallas kernels: 0 us -> 141 us
  blocking collectives: 31.5 us -> 0 us
  matrix products: 16.3 us -> 0 us
  between operations: 13.5 us -> 0.01 us
    all_gather x2 -> x0, waiting for transfers between devices: 182 us -> none  [the longest x1 116 us: shards(): lax.all_gather(u_stack, 'query', axis=0, tiled=True)]
    pallas_call x0 -> x1, Pallas kernels: none -> 141 us  [fused(): pl.pallas_call(functools.partial(kernel, pieces), out_shape=jax.ShapeDtyp...]
    psum x1 -> x0, blocking collectives: 31.5 us -> none  [shards(): return lax.psum(partial_value, 'query')]
    dot_general x2 -> x0, matrix products: 16.3 us -> none  [the longest x1 9.35 us: shards(): jnp.einsum('tkf,kfc->tc', grads_blocks, u_whole, preferred_element_type=j...]
  transfers between devices with their start and end apart: 2 -> 0, of which waited for: 2 -> 0; matrix products, arithmetic and copies ran while one was open for 5% -> 0% of each run, Pallas kernels for 0% -> 0%
where the time goes in v1:
time: 143 us
  Pallas kernels  141 us (99%)
    pallas_call x1, Pallas kernels, fused(): pl.pallas_call(functools.partial(kernel, pieces), out_shape=jax.ShapeDtyp...  141 us

profile of v1, /device:TPU:0, one launch (start us, length us, event | category | flops | bytes accessed | tf_op | source)
XLA Modules:
  0.0 142.7 jit_solution(8645466713743860286)
XLA Ops:
  0.0 141.3 %shard_map.55 = f32[16,2]{1,0:T(8,128)} custom-call(s32[2]{0:T(128)} %lengths.1, bf16[256,14336]{1,0:T(8,128)(2,1)} %grads.1, bf16[256,8192]{1,0:T(8,128)(2,1)} %acts.1, bf16[896,512]{1,0:T(8,128)(2,1)} %u_own.1, bf16[512,512]{1,0:T(8,128)(2,1)} %v_own.1), custom_call_target="tpu_custom_call" | custom-call | flops 5905580032 | bytes 12976128 | tf_op jit(solution)/shard_map/pallas_call | solution.py:231
  141.3 1.3 copy.6

commit v2 on v1

--- a/solution.py
+++ b/solution.py
@@ -95,81 +95,146 @@
     def beside(act, owner, kind):
         act(copy(owner, kind, SIBLING, sibling))
 
+    corner = jnp.logical_or(z == 0, z == DEPTH - 1)
+    inner = jnp.logical_not(corner)
+
     def send_own(act):
-        up, down = z < DEPTH - 1, z > 0
         over(act, me, last)
-        along(act, me, last, up, down)
         for kind in direct:
-            along(act, me, kind, up, down)
+            along(act, me, kind, z < DEPTH - 1, z > 0)
             over(act, me, kind)
         for kind in range(last + 1):
             beside(act, me, kind)
 
-    def send_neighbours(act, wait):
-        wait(across, last)
-        along(act, across, last, z < DEPTH - 1, z > 0)
-        beside(act, across, last)
+    def send_home_turned(act, up, down):
+        along(act, me, last, up, down)
+        along(act, across, last, up, down)
 
     def send_line(act, wait, rank):
         other = nearest(z, rank)
         up = jnp.logical_and(other < z, z < DEPTH - 1)
         down = jnp.logical_and(other > z, z > 0)
-        same, opposite = device(other, y, core), device(other, 1 - y, core)
-        wait(same, last)
-        along(act, same, last, up, down)
-        beside(act, same, last)
+        if act is drain:
+            waits_here = jnp.logical_or(corner, rank < DEPTH - 1)
+            up, down = jnp.logical_and(up, waits_here), jnp.logical_and(down, waits_here)
+        owner = device(other, y, core)
         for kind in direct:
-            wait(same, kind)
-            along(act, same, kind, up, down)
-            over(act, same, kind)
-            beside(act, same, kind)
-        wait(opposite, last)
-        along(act, opposite, last, up, down)
-        beside(act, opposite, last)
+            wait(owner, kind)
+            along(act, owner, kind, up, down)
+            over(act, owner, kind)
+            beside(act, owner, kind)
+
+    def send_turned(act, wait, rank, up, down):
+        other = nearest(z, rank)
+        for owner in (device(other, y, core), device(other, 1 - y, core)):
+            wait(owner, last)
+            along(act, owner, last, up, down)
+            beside(act, owner, last)
 
     def send_crossed(act, wait, rank):
-        opposite = device(nearest(z, rank), 1 - y, core)
+        owner = device(nearest(z, rank), 1 - y, core)
         for kind in direct:
-            wait(opposite, kind)
-            beside(act, opposite, kind)
-
-    def multiply(owner):
-        u_columns = pl.ds(pl.multiple_of(owner * u_rows, 128), u_rows)
-        v_columns = pl.ds(pl.multiple_of(owner * v_rows, 128), v_rows)
-        out_proj[...] += jnp.dot(grads_here[:, u_columns], u_all[owner], preferred_element_type=jnp.float32)
-        in_proj[...] += jnp.dot(acts_here[:, v_columns], v_all[owner], preferred_element_type=jnp.float32)
-
-    def multiply_chip(other_z, other_y):
+            wait(owner, kind)
+            beside(act, owner, kind)
+
+    def wait_long_side():
+        owner = device(nearest(z, DEPTH - 1), y, core)
+        for kind in direct:
+            along(drain, owner, kind, z == 2, z == 1)
+
+    def send_inner_turned(act, wait):
+        send_home_turned(act, z == 1, z == 2)
+        send_turned(act, wait, 1, z == 1, z == 2)
+        if act is start:
+            wait_long_side()
+        send_home_turned(act, z == 2, z == 1)
+
+        @pl.loop(2, DEPTH)
+        def _(rank):
+            send_turned(act, wait, rank, z == 2, z == 1)
+
+    def multiply(owner, kind):
+        side, start_row, size = pieces[kind]
+        own_rows = u_rows if side == 0 else v_rows
+        columns = pl.ds(pl.multiple_of(owner * own_rows + start_row, 128), size)
+        tokens, total = (grads_here, out_proj) if side == 0 else (acts_here, in_proj)
+        total[...] += jnp.dot(tokens[:, columns], piece(owner, kind)[...], preferred_element_type=jnp.float32)
+
+    def multiply_chip(other_z, other_y, kinds):
         @pl.loop(0, CORES)
         def _(turn):
             owner = device(other_z, other_y, jnp.where(turn == 0, core, 1 - core))
 
             @pl.when(turn == 1)
             def _():
-                for kind in range(last + 1):
+                for kind in kinds:
                     arrived(owner, kind)
 
-            multiply(owner)
+            for kind in kinds:
+                multiply(owner, kind)
+
+    def multiply_turned(rank):
+        other = nearest(z, rank)
+        multiply_chip(other, y, (last,))
+        multiply_chip(other, 1 - y, (last,))
 
     loads[0].wait()
     loads[1].wait()
     send_own(start)
     out_proj[...] = jnp.zeros_like(out_proj)
     in_proj[...] = jnp.zeros_like(in_proj)
-    send_neighbours(start, arrived)
     loads[2].wait()
     loads[3].wait()
-    multiply_chip(z, y)
+    multiply_chip(z, y, direct)
+    arrived(across, last)
+    beside(start, across, last)
+
+    def take_crossed(rank):
+        send_crossed(start, arrived, rank)
+        multiply_chip(nearest(z, rank), 1 - y, direct)
 
     @pl.loop(1, DEPTH)
     def _(rank):
         send_line(start, arrived, rank)
-        send_crossed(start, arrived, rank - 1)
-        multiply_chip(nearest(z, rank - 1), 1 - y)
-        multiply_chip(nearest(z, rank), y)
+
+        @pl.when(jnp.logical_and(corner, rank == 1))
+        def _():
+            send_home_turned(start, z == 0, z == DEPTH - 1)
+
+        @pl.when(jnp.logical_and(inner, rank == DEPTH - 1))
+        def _():
+            send_inner_turned(start, arrived)
+
+        behind = jnp.where(corner, rank - 1, rank - 2)
+
+        @pl.when(behind >= 0)
+        def _():
+            take_crossed(behind)
+
+        multiply_chip(nearest(z, rank), y, direct)
+
+    multiply_turned(0)
+
+    @pl.when(inner)
+    def _():
+        take_crossed(DEPTH - 2)
+
+    @pl.loop(1, DEPTH - 1)
+    def _(rank):
+        @pl.when(corner)
+        def _():
+            send_turned(start, arrived, rank, False, False)
+
+        multiply_turned(rank)
 
     send_crossed(start, arrived, DEPTH - 1)
-    multiply_chip(nearest(z, DEPTH - 1), 1 - y)
+
+    @pl.when(corner)
+    def _():
+        send_turned(start, arrived, DEPTH - 1, False, False)
+
+    multiply_chip(nearest(z, DEPTH - 1), 1 - y, direct)
+    multiply_turned(DEPTH - 1)
 
     first_slot = me * rows
     live_count = lengths[first_slot // LENGTH]
@@ -196,7 +261,7 @@
         pass
 
     send_own(drain)
-    send_neighbours(drain, no_wait)
+    beside(drain, across, last)
 
     @pl.loop(1, DEPTH)
     def _(rank):
@@ -205,6 +270,18 @@
     @pl.loop(0, DEPTH)
     def _(rank):
         send_crossed(drain, no_wait, rank)
+
+    @pl.when(corner)
+    def _():
+        send_home_turned(drain, z == 0, z == DEPTH - 1)
+
+        @pl.loop(1, DEPTH)
+        def _(rank):
+            send_turned(drain, no_wait, rank, False, False)
+
+    @pl.when(inner)
+    def _():
+        send_inner_turned(drain, no_wait)
 
     @pl.loop(1, members)
     def _(step):

time: 143 us -> 133 us (0.930)
  Pallas kernels: 141 us -> 131 us
    pallas_call x1, Pallas kernels: 141 us -> 131 us  [fused(): pl.pallas_call(functools.partial(kernel, pieces), out_shape=jax.ShapeDtyp...]
where the time goes in v2:
time: 133 us
  Pallas kernels  131 us (98%)
  local copies, waits for them, and re-layouts  1.33 us (1%)
    pallas_call x1, Pallas kernels, fused(): pl.pallas_call(functools.partial(kernel, pieces), out_shape=jax.ShapeDtyp...  131 us

profile of v2, /device:TPU:0, one launch (start us, length us, event | category | flops | bytes accessed | tf_op | source)
XLA Modules:
  0.0 132.6 jit_solution(250827404130060923)
XLA Ops:
  0.0 131.2 %shard_map.55 = f32[16,2]{1,0:T(8,128)} custom-call(s32[2]{0:T(128)} %lengths.1, bf16[256,14336]{1,0:T(8,128)(2,1)} %grads.1, bf16[256,8192]{1,0:T(8,128)(2,1)} %acts.1, bf16[896,512]{1,0:T(8,128)(2,1)} %u_own.1, bf16[512,512]{1,0:T(8,128)(2,1)} %v_own.1), custom_call_target="tpu_custom_call" | custom-call | flops 5905580032 | bytes 12976128 | tf_op jit(solution)/shard_map/pallas_call | solution.py:308
  131.2 1.3 %copy.6 = f32[16,2]{0,1:T(2,128)} copy(f32[16,2]{1,0:T(8,128)} %shard_map.55) | data formatting | bytes 256 | tf_op jit(solution)/shard_map/pallas_call | solution.py:308

commit v3 on v2

--- a/solution.py
+++ b/solution.py
@@ -12,6 +12,7 @@
 MESH = pl.DeviceIdType.MESH
 DEPTH, WIDTH, CORES = 4, 2, 2
 UP, DOWN, ACROSS, SIBLING = range(4)
+LENT_CHUNKS = 2
 
 
 def device(z, y, core):
@@ -26,7 +27,8 @@
 
 
 def kernel(pieces, lengths, grads, acts, u_own, v_own, out, u_all, v_all, grads_here, acts_here, out_proj, in_proj,
-           parts, load_sem, send_sem, recv_sem, part_send_sem, part_recv_sem):
+           acts_lent, part_lent, part_back, parts, load_sem, send_sem, recv_sem, lend_sem, back_sem,
+           part_send_sem, part_recv_sem):
     me = lax.axis_index("query")
     members = u_all.shape[0]
     core = lax.rem(me, CORES)
@@ -77,8 +79,7 @@
     def arrived(owner, kind):
         copy(owner, kind, SIBLING, sibling).wait_recv()
 
-    last = len(pieces) - 1
-    direct = tuple(range(last))
+    direct, turned = (0, 1), (2, 3)
 
     def along(act, owner, kind, up, down):
         @pl.when(up)
@@ -99,24 +100,27 @@
     inner = jnp.logical_not(corner)
 
     def send_own(act):
-        over(act, me, last)
+        for kind in turned:
+            over(act, me, kind)
         for kind in direct:
             along(act, me, kind, z < DEPTH - 1, z > 0)
             over(act, me, kind)
-        for kind in range(last + 1):
+        for kind in direct + turned:
             beside(act, me, kind)
 
-    def send_home_turned(act, up, down):
-        along(act, me, last, up, down)
-        along(act, across, last, up, down)
+    def wait_own_along():
+        for kind in direct:
+            along(drain, me, kind, z == 0, z == DEPTH - 1)
+
+    def send_home_turned(act):
+        for owner in (me, across):
+            for kind in turned:
+                along(act, owner, kind, z < 2, z >= 2)
 
     def send_line(act, wait, rank):
         other = nearest(z, rank)
         up = jnp.logical_and(other < z, z < DEPTH - 1)
         down = jnp.logical_and(other > z, z > 0)
-        if act is drain:
-            waits_here = jnp.logical_or(corner, rank < DEPTH - 1)
-            up, down = jnp.logical_and(up, waits_here), jnp.logical_and(down, waits_here)
         owner = device(other, y, core)
         for kind in direct:
             wait(owner, kind)
@@ -127,9 +131,10 @@
     def send_turned(act, wait, rank, up, down):
         other = nearest(z, rank)
         for owner in (device(other, y, core), device(other, 1 - y, core)):
-            wait(owner, last)
-            along(act, owner, last, up, down)
-            beside(act, owner, last)
+            for kind in turned:
+                wait(owner, kind)
+                along(act, owner, kind, up, down)
+                beside(act, owner, kind)
 
     def send_crossed(act, wait, rank):
         owner = device(nearest(z, rank), 1 - y, core)
@@ -137,21 +142,47 @@
             wait(owner, kind)
             beside(act, owner, kind)
 
-    def wait_long_side():
-        owner = device(nearest(z, DEPTH - 1), y, core)
-        for kind in direct:
-            along(drain, owner, kind, z == 2, z == 1)
-
-    def send_inner_turned(act, wait):
-        send_home_turned(act, z == 1, z == 2)
-        send_turned(act, wait, 1, z == 1, z == 2)
-        if act is start:
-            wait_long_side()
-        send_home_turned(act, z == 2, z == 1)
-
-        @pl.loop(2, DEPTH)
-        def _(rank):
-            send_turned(act, wait, rank, z == 2, z == 1)
+    inward = device(jnp.where(z < 2, z + 1, z - 1), y, core)
+    outward = device(jnp.where(z < 2, z - 1, z + 1), y, core)
+    first_lent = CORES * WIDTH
+    lent = members - 2 * first_lent
+    lent_rows = rows // LENT_CHUNKS
+
+    def lend(chunk):
+        here = pl.ds(chunk * lent_rows, lent_rows)
+        return pltpu.make_async_remote_copy(
+            src_ref=acts_here.at[here, pl.ds(first_lent * v_rows, lent * v_rows)],
+            dst_ref=acts_lent.at[here],
+            send_sem=lend_sem.at[0, chunk],
+            recv_sem=lend_sem.at[1, chunk],
+            device_id={"query": inward},
+            device_id_type=MESH,
+        )
+
+    def give_back(chunk):
+        here = pl.ds(chunk * lent_rows, lent_rows)
+        return pltpu.make_async_remote_copy(
+            src_ref=part_lent.at[here],
+            dst_ref=part_back.at[here],
+            send_sem=back_sem.at[0, chunk],
+            recv_sem=back_sem.at[1, chunk],
+            device_id={"query": outward},
+            device_id_type=MESH,
+        )
+
+    def work_lent(chunk):
+        here = pl.ds(chunk * lent_rows, lent_rows)
+        lend(chunk).wait_recv()
+        part_lent[here] = jnp.zeros((lent_rows, part_lent.shape[1]), jnp.float32)
+
+        @pl.loop(0, lent)
+        def _(turn):
+            columns = pl.ds(pl.multiple_of(turn * v_rows, 128), v_rows)
+            part_lent[here] += jnp.dot(
+                acts_lent[here, columns], v_all[first_lent + turn], preferred_element_type=jnp.float32
+            )
+
+        give_back(chunk).start()
 
     def multiply(owner, kind):
         side, start_row, size = pieces[kind]
@@ -175,8 +206,8 @@
 
     def multiply_turned(rank):
         other = nearest(z, rank)
-        multiply_chip(other, y, (last,))
-        multiply_chip(other, 1 - y, (last,))
+        multiply_chip(other, y, turned)
+        multiply_chip(other, 1 - y, turned)
 
     loads[0].wait()
     loads[1].wait()
@@ -186,8 +217,9 @@
     loads[2].wait()
     loads[3].wait()
     multiply_chip(z, y, direct)
-    arrived(across, last)
-    beside(start, across, last)
+    for kind in turned:
+        arrived(across, kind)
+        beside(start, across, kind)
 
     def take_crossed(rank):
         send_crossed(start, arrived, rank)
@@ -199,13 +231,25 @@
 
         @pl.when(jnp.logical_and(corner, rank == 1))
         def _():
-            send_home_turned(start, z == 0, z == DEPTH - 1)
-
-        @pl.when(jnp.logical_and(inner, rank == DEPTH - 1))
-        def _():
-            send_inner_turned(start, arrived)
-
-        behind = jnp.where(corner, rank - 1, rank - 2)
+            wait_own_along()
+            send_home_turned(start)
+
+        @pl.when(jnp.logical_and(corner, rank == 2))
+        def _():
+            send_home_turned(drain)
+            lend(0).start()
+
+        @pl.when(jnp.logical_and(corner, rank == 3))
+        def _():
+            for chunk in range(1, LENT_CHUNKS):
+                lend(chunk - 1).wait_send()
+                lend(chunk).start()
+
+        @pl.when(jnp.logical_and(inner, rank == 3))
+        def _():
+            send_home_turned(start)
+
+        behind = jnp.where(corner, rank - 1, rank - 3)
 
         @pl.when(behind >= 0)
         def _():
@@ -217,15 +261,17 @@
 
     @pl.when(inner)
     def _():
-        take_crossed(DEPTH - 2)
-
-    @pl.loop(1, DEPTH - 1)
-    def _(rank):
-        @pl.when(corner)
-        def _():
-            send_turned(start, arrived, rank, False, False)
-
-        multiply_turned(rank)
+        send_home_turned(drain)
+        send_turned(start, arrived, 1, z == 1, z == 2)
+        send_turned(start, arrived, 2, False, False)
+        multiply_turned(2)
+        for chunk in range(LENT_CHUNKS - 1):
+            work_lent(chunk)
+        send_turned(start, arrived, 3, z == 2, z == 1)
+        work_lent(LENT_CHUNKS - 1)
+        take_crossed(1)
+        take_crossed(2)
+        multiply_turned(1)
 
     send_crossed(start, arrived, DEPTH - 1)
 
@@ -235,6 +281,12 @@
 
     multiply_chip(nearest(z, DEPTH - 1), 1 - y, direct)
     multiply_turned(DEPTH - 1)
+
+    @pl.when(corner)
+    def _():
+        for chunk in range(LENT_CHUNKS):
+            give_back(chunk).wait_recv()
+        in_proj[...] += part_back[...]
 
     first_slot = me * rows
     live_count = lengths[first_slot // LENGTH]
@@ -260,8 +312,15 @@
     def no_wait(owner, kind):
         pass
 
-    send_own(drain)
-    beside(drain, across, last)
+    for kind in turned:
+        over(drain, me, kind)
+    for kind in direct:
+        along(drain, me, kind, inner, inner)
+        over(drain, me, kind)
+    for kind in direct + turned:
+        beside(drain, me, kind)
+    for kind in turned:
+        beside(drain, across, kind)
 
     @pl.loop(1, DEPTH)
     def _(rank):
@@ -273,15 +332,16 @@
 
     @pl.when(corner)
     def _():
-        send_home_turned(drain, z == 0, z == DEPTH - 1)
-
-        @pl.loop(1, DEPTH)
-        def _(rank):
-            send_turned(drain, no_wait, rank, False, False)
+        send_turned(drain, no_wait, DEPTH - 1, False, False)
+        lend(LENT_CHUNKS - 1).wait_send()
 
     @pl.when(inner)
     def _():
-        send_inner_turned(drain, no_wait)
+        send_turned(drain, no_wait, 1, z == 1, z == 2)
+        send_turned(drain, no_wait, 2, False, False)
+        send_turned(drain, no_wait, 3, z == 2, z == 1)
+        for chunk in range(LENT_CHUNKS):
+            give_back(chunk).wait_send()
 
     @pl.loop(1, members)
     def _(step):
@@ -317,10 +377,15 @@
             pltpu.VMEM(acts.shape, acts.dtype),
             pltpu.VMEM((rows, factor_cols), jnp.float32),
             pltpu.VMEM((rows, factor_cols), jnp.float32),
+            pltpu.VMEM((rows, (members - 2 * CORES * WIDTH) * v_rows), acts.dtype),
+            pltpu.VMEM((rows, factor_cols), jnp.float32),
+            pltpu.VMEM((rows, factor_cols), jnp.float32),
             pltpu.VMEM((members, 1, factor_cols), jnp.float32),
             pltpu.SemaphoreType.DMA((4,)),
             pltpu.SemaphoreType.DMA((4, members, len(pieces))),
             pltpu.SemaphoreType.DMA((members, len(pieces))),
+            pltpu.SemaphoreType.DMA((2, LENT_CHUNKS)),
+            pltpu.SemaphoreType.DMA((2, LENT_CHUNKS)),
             pltpu.SemaphoreType.DMA((members,)),
             pltpu.SemaphoreType.DMA((members,)),
         ],

time: 133 us -> 122 us (0.917)
  Pallas kernels: 131 us -> 121 us
    pallas_call x1, Pallas kernels: 131 us -> 121 us  [fused(): pl.pallas_call(functools.partial(kernel, pieces), out_shape=jax.ShapeDtyp...]
where the time goes in v3:
time: 122 us
  Pallas kernels  121 us (99%)
  local copies, waits for them, and re-layouts  1.33 us (1%)
    pallas_call x1, Pallas kernels, fused(): pl.pallas_call(functools.partial(kernel, pieces), out_shape=jax.ShapeDtyp...  121 us

profile of v3, /device:TPU:0, one launch (start us, length us, event | category | flops | bytes accessed | tf_op | source)
XLA Modules:
  0.0 121.9 jit_solution(11791739304145207705)
XLA Ops:
  0.0 120.6 %shard_map.55 = f32[16,2]{1,0:T(8,128)} custom-call(s32[2]{0:T(128)} %lengths.1, bf16[256,14336]{1,0:T(8,128)(2,1)} %grads.1, bf16[256,8192]{1,0:T(8,128)(2,1)} %acts.1, bf16[896,512]{1,0:T(8,128)(2,1)} %u_own.1, bf16[512,512]{1,0:T(8,128)(2,1)} %v_own.1), custom_call_target="tpu_custom_call" | custom-call | flops 5905580032 | bytes 12976128 | tf_op jit(solution)/shard_map/pallas_call | solution.py:368
  120.6 1.3 %copy.6 = f32[16,2]{0,1:T(2,128)} copy(f32[16,2]{1,0:T(8,128)} %shard_map.55) | data formatting | bytes 256 | tf_op jit(solution)/shard_map/pallas_call | solution.py:368

commit v4 on v3

--- a/solution.py
+++ b/solution.py
@@ -79,7 +79,7 @@
     def arrived(owner, kind):
         copy(owner, kind, SIBLING, sibling).wait_recv()
 
-    direct, turned = (0, 1), (2, 3)
+    direct, turned = (0,), (1,)
 
     def along(act, owner, kind, up, down):
         @pl.when(up)
@@ -142,6 +142,12 @@
             wait(owner, kind)
             beside(act, owner, kind)
 
+    def wait_corner_turned():
+        other = nearest(z, 1)
+        for owner in (device(other, y, core), device(other, 1 - y, core)):
+            for kind in turned:
+                along(drain, owner, kind, z == 1, z == 2)
+
     inward = device(jnp.where(z < 2, z + 1, z - 1), y, core)
     outward = device(jnp.where(z < 2, z - 1, z + 1), y, core)
     first_lent = CORES * WIDTH
@@ -217,9 +223,11 @@
     loads[2].wait()
     loads[3].wait()
     multiply_chip(z, y, direct)
-    for kind in turned:
-        arrived(across, kind)
-        beside(start, across, kind)
+
+    def take_neighbours_turned():
+        for kind in turned:
+            arrived(across, kind)
+            beside(start, across, kind)
 
     def take_crossed(rank):
         send_crossed(start, arrived, rank)
@@ -232,6 +240,7 @@
         @pl.when(jnp.logical_and(corner, rank == 1))
         def _():
             wait_own_along()
+            take_neighbours_turned()
             send_home_turned(start)
 
         @pl.when(jnp.logical_and(corner, rank == 2))
@@ -247,7 +256,8 @@
 
         @pl.when(jnp.logical_and(inner, rank == 3))
         def _():
-            send_home_turned(start)
+            take_neighbours_turned()
+            send_turned(start, arrived, 1, z == 1, z == 2)
 
         behind = jnp.where(corner, rank - 1, rank - 3)
 
@@ -261,17 +271,33 @@
 
     @pl.when(inner)
     def _():
-        send_home_turned(drain)
-        send_turned(start, arrived, 1, z == 1, z == 2)
+        wait_corner_turned()
+        send_home_turned(start)
+        send_turned(start, arrived, 3, z == 2, z == 1)
         send_turned(start, arrived, 2, False, False)
         multiply_turned(2)
-        for chunk in range(LENT_CHUNKS - 1):
+        for chunk in range(LENT_CHUNKS):
             work_lent(chunk)
-        send_turned(start, arrived, 3, z == 2, z == 1)
-        work_lent(LENT_CHUNKS - 1)
         take_crossed(1)
         take_crossed(2)
         multiply_turned(1)
+
+    def no_wait(owner, kind):
+        pass
+
+    for kind in turned:
+        over(drain, me, kind)
+    for kind in direct:
+        along(drain, me, kind, inner, inner)
+        over(drain, me, kind)
+    for kind in direct + turned:
+        beside(drain, me, kind)
+    for kind in turned:
+        beside(drain, across, kind)
+
+    send_line(drain, no_wait, 1)
+    send_crossed(drain, no_wait, 0)
+    send_crossed(drain, no_wait, 1)
 
     send_crossed(start, arrived, DEPTH - 1)
 
@@ -309,24 +335,11 @@
     def _(step):
         part_copy(step).start()
 
-    def no_wait(owner, kind):
-        pass
-
-    for kind in turned:
-        over(drain, me, kind)
-    for kind in direct:
-        along(drain, me, kind, inner, inner)
-        over(drain, me, kind)
-    for kind in direct + turned:
-        beside(drain, me, kind)
-    for kind in turned:
-        beside(drain, across, kind)
-
-    @pl.loop(1, DEPTH)
+    @pl.loop(2, DEPTH)
     def _(rank):
         send_line(drain, no_wait, rank)
 
-    @pl.loop(0, DEPTH)
+    @pl.loop(2, DEPTH)
     def _(rank):
         send_crossed(drain, no_wait, rank)
 
@@ -337,7 +350,8 @@
 
     @pl.when(inner)
     def _():
-        send_turned(drain, no_wait, 1, z == 1, z == 2)
+        send_home_turned(drain)
+        send_turned(drain, no_wait, 1, False, False)
         send_turned(drain, no_wait, 2, False, False)
         send_turned(drain, no_wait, 3, z == 2, z == 1)
         for chunk in range(LENT_CHUNKS):
@@ -361,9 +375,7 @@
     members = lax.axis_size("query")
     rows, factor_cols = acts.shape[0], u_factor.shape[1]
     u_rows, v_rows = u_factor.shape[0], v_factor.shape[0]
-    u_cut = -(-u_rows // 256) * 128
-    v_cut = v_rows // 256 * 128
-    pieces = ((0, 0, u_cut), (0, u_cut, u_rows - u_cut), (1, 0, v_cut), (1, v_cut, v_rows - v_cut))
+    pieces = ((0, 0, u_rows), (1, 0, v_rows))
     hbm = pl.BlockSpec(memory_space=pl.ANY)
     return pl.pallas_call(
         functools.partial(kernel, pieces),

time: 122 us -> 119 us (0.975)
  Pallas kernels: 121 us -> 117 us
    pallas_call x1, Pallas kernels: 121 us -> 117 us  [fused(): pl.pallas_call(functools.partial(kernel, pieces), out_shape=jax.ShapeDtyp...]
where the time goes in v4:
time: 119 us
  Pallas kernels  117 us (98%)
  local copies, waits for them, and re-layouts  1.33 us (1%)
    pallas_call x1, Pallas kernels, fused(): pl.pallas_call(functools.partial(kernel, pieces), out_shape=jax.ShapeDtyp...  117 us

profile of v4, /device:TPU:0, one launch (start us, length us, event | category | flops | bytes accessed | tf_op | source)
XLA Modules:
  0.0 118.7 jit_solution(5342774136144211093)
XLA Ops:
  0.0 117.4 %shard_map.55 = f32[16,2]{1,0:T(8,128)} custom-call(s32[2]{0:T(128)} %lengths.1, bf16[256,14336]{1,0:T(8,128)(2,1)} %grads.1, bf16[256,8192]{1,0:T(8,128)(2,1)} %acts.1, bf16[896,512]{1,0:T(8,128)(2,1)} %u_own.1, bf16[512,512]{1,0:T(8,128)(2,1)} %v_own.1), custom_call_target="tpu_custom_call" | custom-call | flops 5905580032 | bytes 12976128 | tf_op jit(solution)/shard_map/pallas_call | solution.py:380
  117.4 1.3 %copy.6 = f32[16,2]{0,1:T(2,128)} copy(f32[16,2]{1,0:T(8,128)} %shard_map.55) | data formatting | bytes 256 | tf_op jit(solution)/shard_map/pallas_call | solution.py:380
